TPU v7x, 128 devices: a whole 4x4x4 slice. The times are simulated.
128 devices in a mesh: row: 8 (over y, x_hi), col: 16 (over z, x_lo, core).
Axes of the slice: x: 4 (x_hi: 2, x_lo: 2; x = x_hi * 2 + x_lo), y: 4, z: 4, core: 2. Of those that a mesh axis runs over, the one named last changes fastest.
Arguments:
- momentum: float32 [16384, 16384], P(('row', 'col')), may hold values from -1200 to 1200
Outputs:
- gram: float32 [16384, 16384], P('row', 'col')
- tiles: bfloat16 [16384, 16384], P('row', 'col')
All inputs are finite; a program needn't handle non-finite values.
Results may differ from a plain program's by a relative error of at most 0.0043.
Values may be sent and summed in bfloat16 or wider, within the bound.
A program may use at most 128 MiB of HBM per device.

v0:
```python
import jax
import jax.numpy as jnp
from jax import lax
from jax.sharding import PartitionSpec as P

STEPS = 2


def spread(value, axis, source):
    kept = jnp.where(lax.axis_index(axis) == source, value, 0).astype(value.dtype)
    return lax.psum(kept, axis)


def panel_product(panel, columns):
    return lax.dot_general(
        panel, columns, (((1,), (1,)), ((), ())), preferred_element_type=jnp.float32
    )


def shards(momentum):
    n_row = lax.axis_size("row")
    n_col = lax.axis_size("col")
    partial_sum = jnp.sum(momentum * momentum)
    total = lax.psum(partial_sum, ("row", "col"))
    scale = 1.0 / (jnp.sqrt(total) + 1e-07)
    scaled = (momentum * scale).astype(jnp.bfloat16)
    tiles = lax.all_to_all(scaled, "col", split_axis=1, concat_axis=0, tiled=True)
    ratio = n_col // n_row
    width = tiles.shape[1]
    col_place = lax.axis_index("col")
    source_row = col_place // ratio
    offset = col_place % ratio * width
    gram = jnp.zeros((tiles.shape[0], width), jnp.float32)
    for step in range(STEPS):
        panel = spread(tiles, "col", step)
        own_rows = lax.dynamic_slice_in_dim(panel, offset, width, 0)
        columns = spread(own_rows, "row", source_row)
        gram = gram + panel_product(panel, columns)
    return (gram * jnp.float32(width * n_col), tiles)


def solution(mesh):
    return jax.shard_map(
        shards,
        mesh=mesh,
        in_specs=(P(("row", "col"), None),),
        out_specs=(P("row", "col"), P("row", "col")),
        check_vma=False,
    )
```

profile of v0, /device:TPU:19, one launch (start us, length us, event | category | flops | bytes accessed | tf_op | source)
XLA Modules:
  0.0 555.9 jit_solution(7661064828272330656)
XLA Ops:
  7.2 6.1 %multiply_reduce_fusion = f32[]{:T(128)} fusion(f32[128,16384]{1,0:T(8,128)} %param.1), kind=kLoop, calls=%fused_computation.2 | loop fusion | flops 4194303 | bytes 8388612 | tf_op jit(solution)/shard_map/reduce_sum | solution.py:23
  13.3 65.2 %psum.35 = f32[]{:T(128)} all-reduce(f32[]{:T(128)} %multiply_reduce_fusion), channel_id=1, replica_groups=mesh['row'=8,'col'=16] {'row','col'}, use_global_device_ids=true, to_apply=%region_1.0 | all-reduce | flops 1 | bytes 8 | tf_op jit(solution)/shard_map/psum | solution.py:24
  79.2 4.0 multiply_convert_fusion
  83.2 2.5 copy.6
  85.7 6.2 %all-to-all-start = ((bf16[128,16,1024]{2,0,1:T(8,128)(2,1)}), bf16[128,16,1024]{2,0,1:T(8,128)(2,1)}, u32[]{:S(2)}, u32[]{:S(2)}) async-start(bf16[128,16,1024]{2,0,1:T(8,128)(2,1)} %bitcast.12), calls=%async_computation | async-start | bytes 8388608 | tf_op jit(solution)/shard_map/all_to_all | solution.py:27
  91.9 0.0 all-reduce.5.cloned.1.call-start
  92.0 49.2 %all-to-all-done = bf16[128,16,1024]{2,0,1:T(8,128)(2,1)} async-done(((bf16[128,16,1024]{2,0,1:T(8,128)(2,1)}), bf16[128,16,1024]{2,0,1:T(8,128)(2,1)}, u32[]{:S(2)}, u32[]{:S(2)}) %all-to-all-start) | async-done | bytes 4194336 | tf_op jit(solution)/shard_map/all_to_all | solution.py:27
  141.1 6.1 %broadcast_select_fusion = (bf16[2048,1024]{1,0:T(8,128)(2,1)}, bf16[2048,1024]{1,0:T(8,128)(2,1)}) fusion(pred[]{:T(512)S(6)} %eq.14, pred[]{:T(512)S(6)} %eq.12, bf16[128,16,1024]{2,0,1:T(8,128)(2,1)} %all-to-all-done), kind=kLoop, calls=%fused_computation.4 | loop fusion | flops 4194304 | bytes 12582914 | tf_op jit(solution)/shard_map/jit(_where)/select_n | solution.py:10
  147.3 0.0 all-reduce.5.cloned.1.call-update
  147.3 0.0 all-reduce.7.cloned.1.call-start
  147.4 192.8 %all-reduce.5.cloned.1.call-done = (bf16[2048,1024]{1,0:T(8,128)(2,1)}, bf16[2048,1024]{1,0:T(8,128)(2,1)}) async-done(((bf16[2048,1024]{1,0:T(8,128)(2,1)}, bf16[2048,1024]{1,0:T(8,128)(2,1)}), (bf16[2048,1024]{1,0:T(8,128)(2,1)}, bf16[2048,1024]{1,0:T(8,128)(2,1)})) %all-reduce.5.cloned.1.call-update) | async-done | bytes 8388624 | tf_op jit(solution)/shard_map/psum | solution.py:11
  340.2 5.5 dynamic-slice_select_fusion
  345.7 0.0 all-reduce.7.cloned.1.call-update
  345.7 184.4 %all-reduce.7.cloned.1.call-done = (bf16[1024,1024]{1,0:T(8,128)(2,1)}, bf16[1024,1024]{1,0:T(8,128)(2,1)}) async-done(((bf16[1024,1024]{1,0:T(8,128)(2,1)}, bf16[1024,1024]{1,0:T(8,128)(2,1)}), (bf16[1024,1024]{1,0:T(8,128)(2,1)}, bf16[1024,1024]{1,0:T(8,128)(2,1)})) %all-reduce.7.cloned.1.call-update) | async-done | bytes 4194320 | tf_op jit(solution)/shard_map/psum | solution.py:11
  530.1 0.0 copy-start
  530.1 0.0 copy-start.1
  530.1 7.1 %fusion = f32[2048,1024]{1,0:T(8,128)S(1)} fusion(bf16[2048,1024]{1,0:T(8,128)(2,1)} %get-tuple-element.2, bf16[1024,1024]{1,0:T(8,128)(2,1)} %get-tuple-element.4), kind=kOutput, calls=%fused_computation.8 | convolution fusion | flops 4294967296 | bytes 14680064 | tf_op jit(solution)/shard_map/dot_general | solution.py:15
  537.3 0.0 copy-done
  537.3 0.0 copy-done.1
  537.3 7.2 %add_multiply_fusion = f32[2048,1024]{1,0:T(8,128)} fusion(f32[2048,1024]{1,0:T(8,128)S(1)} %fusion, bf16[2048,1024]{1,0:T(8,128)(2,1)S(1)} %copy-done, bf16[1024,1024]{1,0:T(8,128)(2,1)S(1)} %copy-done.1), kind=kOutput, calls=%fused_computation | convolution fusion | flops 4299161600 | bytes 23068672 | tf_op jit(solution)/shard_map/dot_general | solution.py:15
  544.5 4.6 copy.12
Async XLA Ops:
  85.7 55.5 %all-to-all-start = ((bf16[128,16,1024]{2,0,1:T(8,128)(2,1)}), bf16[128,16,1024]{2,0,1:T(8,128)(2,1)}, u32[]{:S(2)}, u32[]{:S(2)}) async-start(bf16[128,16,1024]{2,0,1:T(8,128)(2,1)} %bitcast.12), calls=%async_computation | async-start | bytes 8388608 | tf_op jit(solution)/shard_map/all_to_all | solution.py:27
  91.9 248.3 %all-reduce.5.cloned.1.call-start = ((), (), s32[]{:S(2)}) async-start(), calls=%async_computation.1 | async-start | bytes 16777216 | tf_op jit(solution)/shard_map/psum | solution.py:11
  147.3 382.8 %all-reduce.7.cloned.1.call-start = ((), (), s32[]{:S(2)}) async-start(), calls=%async_computation.2 | async-start | bytes 8388608 | tf_op jit(solution)/shard_map/psum | solution.py:11
  530.1 7.2 %copy-start = (bf16[2048,1024]{1,0:T(8,128)(2,1)S(1)}, bf16[2048,1024]{1,0:T(8,128)(2,1)}, u32[]{:S(2)}) copy-start(bf16[2048,1024]{1,0:T(8,128)(2,1)} %get-tuple-element.3) | copy-start | bytes 12582916
  530.1 7.2 %copy-start.1 = (bf16[1024,1024]{1,0:T(8,128)(2,1)S(1)}, bf16[1024,1024]{1,0:T(8,128)(2,1)}, u32[]{:S(2)}) copy-start(bf16[1024,1024]{1,0:T(8,128)(2,1)} %get-tuple-element.5) | copy-start | bytes 6291460
Sparse Core Ops, SparseCore 0:
  147.4 192.7 all-reduce.4
  345.9 184.2 all-reduce.6
where the time goes:
time: 559 us; the launch traced here: 556 us
  waiting for transfers between devices  426 us (76%)
  blocking collectives  65.2 us (12%)
  other arithmetic  21.7 us (4%)
  between operations  14.8 us (3%)
  matrix products  14.3 us (3%)
  local copies, waits for them, and re-layouts  7.14 us (1%)
  starting transfers between devices  6.33 us (1%)
    psum x2, waiting for transfers between devices, spread(): return lax.psum(kept, axis)  377 us
    psum x1, blocking collectives, shards(): total = lax.psum(partial_sum, ('row', 'col'))  65.2 us
    all_to_all x1, waiting for transfers between devices, shards(): lax.all_to_all(scaled, 'col', split_axis=1, concat_axis=0, tiled=True)  49.2 us
    dot_general x2, matrix products, panel_product(): lax.dot_general(panel, columns, (((1,), (1,)), ((), ())), preferred_eleme...  14.3 us
    select_n x2, other arithmetic, spread(): jnp.where(lax.axis_index(axis) == source, value, 0).astype(value.dtype)  11.6 us
  transfers between devices with their start and end apart: 3, of which 3 were waited for; matrix products, arithmetic and copies ran while one was open for 0% of the time, Pallas kernels for 0%

commit v1 on v0

v1 whole, which is shorter than its diff:
```python
import jax
import jax.numpy as jnp
from jax import lax
from jax.experimental import pallas as pl
from jax.experimental.pallas import tpu as pltpu
from jax.sharding import PartitionSpec as P

MESH = pl.DeviceIdType.MESH
BF16 = jnp.bfloat16
F32 = jnp.float32

COLS = 16
ROWS = 8
SHARD = 128
WIDTH = 1024
WINDOW = 2048
SUB = 64
MIB = 1 << 20
ISSUE = (2, 2, 2, 2, 2, 2, 2, 1)


def nothing(*_):
    return 0


def kernel(
    m_ref, gram_ref, tiles_ref,
    held, coded, panel, columns, sums1, sums2,
    load_sem, s1_send, s1_recv, s2_send, s2_recv,
    t_send, t_recv, r_send, r_recv, o_send, c_send, c_recv, local_sem,
):
    row = lax.axis_index("row")
    col = lax.axis_index("col")
    y, xh = row // 2, row % 2
    z, xl, core = col // 4, (col // 2) % 2, col % 2
    other = 1 - core
    up, down = (z + 1) % 4, (z + 3) % 4
    even = xh == xl
    turn = (y - z + 4) % 4
    home = turn == 0

    def place(y_, xh_, z_, xl_, core_):
        return (y_ * 2 + xh_, z_ * 4 + xl_ * 2 + core_)

    cross = place(y, 1 - xh, z, 1 - xl, core)

    def load(j):
        part = pl.ds(pl.multiple_of(j * 2 * WIDTH, 2 * WIDTH), 2 * WIDTH)
        return pltpu.make_async_copy(m_ref.at[:, part], held.at[:, part], load_sem.at[j])

    for j in range(8):
        load(j).start()

    barrier = pltpu.get_barrier_semaphore()

    def greet_col(i, _):
        pl.semaphore_signal(barrier, inc=1, device_id=(row, (col + i) % COLS), device_id_type=MESH)
        return 0

    def greet_row(i, _):
        pl.semaphore_signal(barrier, inc=1, device_id=((row + i) % ROWS, col), device_id_type=MESH)
        return 0

    lax.fori_loop(1, COLS, greet_col, 0)
    lax.fori_loop(1, ROWS, greet_row, 0)
    pl.semaphore_signal(barrier, inc=1, device_id=cross, device_id_type=MESH)

    def square(j, total):
        load(j).wait()
        part = held[:, pl.ds(pl.multiple_of(j * 2 * WIDTH, 2 * WIDTH), 2 * WIDTH)]
        part = (part * part).reshape(SHARD // 8, 8, 2 * WIDTH).sum(axis=0)
        for k in range(2 * WIDTH // 128):
            total = total + part[:, k * 128 : (k + 1) * 128]
        return total

    sums1[col] = lax.fori_loop(0, 8, square, jnp.zeros((8, 128), F32))

    pl.semaphore_wait(barrier, COLS + ROWS - 1)

    def send1(i):
        to = (col + i) % COLS
        return pltpu.make_async_remote_copy(
            src_ref=sums1.at[col], dst_ref=sums1.at[col], send_sem=s1_send.at[i], recv_sem=s1_recv.at[col],
            device_id=(row, to), device_id_type=MESH,
        )

    def recv1(i):
        source = (col + i) % COLS
        return pltpu.make_async_remote_copy(
            src_ref=sums1.at[source], dst_ref=sums1.at[source], send_sem=s1_send.at[i], recv_sem=s1_recv.at[source],
            device_id=(row, source), device_id_type=MESH,
        )

    def send2(i):
        to = (row + i) % ROWS
        return pltpu.make_async_remote_copy(
            src_ref=sums2.at[row], dst_ref=sums2.at[row], send_sem=s2_send.at[i], recv_sem=s2_recv.at[row],
            device_id=(to, col), device_id_type=MESH,
        )

    def recv2(i):
        source = (row + i) % ROWS
        return pltpu.make_async_remote_copy(
            src_ref=sums2.at[source], dst_ref=sums2.at[source], send_sem=s2_send.at[i], recv_sem=s2_recv.at[source],
            device_id=(source, col), device_id_type=MESH,
        )

    def each(low, high, act):
        def body(i, _):
            act(i)
            return 0

        lax.fori_loop(low, high, body, 0)

    each(1, COLS, lambda i: send1(i).start())
    each(1, COLS, lambda i: recv1(i).wait_recv())
    group = sums1[0]
    for k in range(1, COLS):
        group = group + sums1[k]
    sums2[row] = group
    each(1, ROWS, lambda i: send2(i).start())
    each(1, ROWS, lambda i: recv2(i).wait_recv())
    whole = sums2[0]
    for k in range(1, ROWS):
        whole = whole + sums2[k]
    total = jnp.sum(jnp.sum(whole, axis=0, keepdims=True), axis=1, keepdims=True)
    scale = 1.0 / (jnp.sqrt(total) + 1e-07)

    own = pl.multiple_of(col * SHARD, SHARD)
    panel[pl.ds(own, SHARD), :] = (held[:, :WINDOW] * scale).astype(BF16)

    def piece(block, s):
        return pl.ds(pl.multiple_of(block * SHARD + s * SUB, SUB), SUB)

    def pass_on(block, s, slot, target):
        return pltpu.make_async_remote_copy(
            src_ref=panel.at[piece(block, s)], dst_ref=panel.at[piece(block, s)],
            send_sem=r_send.at[slot, s], recv_sem=r_recv.at[block, s], device_id=target, device_id_type=MESH,
        )

    def arrived(block, s):
        pass_on(block, s, 0, (row, col)).wait_recv()

    def name(z_, xl_, core_):
        return z_ * 4 + xl_ * 2 + core_

    above = place(y, xh, up, xl, core)
    below = place(y, xh, down, xl, core)
    beside = place(y, xh, z, 1 - xl, core)
    sibling = place(y, xh, z, xl, other)

    def start_of(j):
        far = jnp.where(j < 6, 1, 3)
        return jnp.where(even | (j < 4), 0, far)

    def way_of(j):
        e = jnp.where(j < 4, 1, 3)
        m = jnp.where(j < 4, jnp.where(j < 2, 1, 3), jnp.where(j % 2 == 0, 1, 3))
        return jnp.where(even, e, m)

    def lead(block, s):
        j = block % 8
        near = (1 - xh, 1 - xl)
        step = jnp.where(even, way_of(j), start_of(j))
        direct = jnp.logical_not(even) & (j < 4)
        slot = jnp.where(even | (j < 4), j, 8 + j % 2)
        target = place(
            (y + step) % 4, jnp.where(direct, near[0], xh), z, jnp.where(direct, near[1], xl), core
        )
        return pltpu.make_async_remote_copy(
            src_ref=panel.at[piece(block, s)], dst_ref=columns.at[piece(slot, s)],
            send_sem=o_send.at[j, s], recv_sem=c_recv.at[slot, s], device_id=target, device_id_type=MESH,
        )

    def keep(block, s):
        return pltpu.make_async_copy(
            panel.at[piece(block, s)], columns.at[piece(block % 8, s)], local_sem.at[block % 8, s]
        )

    def have(block, s):
        @pl.when(home & (block // 8 == core))
        def _():
            lead(block, s).start()

            @pl.when(even)
            def _():
                keep(block, s).start()

    def tile_send(i):
        to = (col + i) % COLS
        return pltpu.make_async_remote_copy(
            src_ref=coded.at[to], dst_ref=tiles_ref.at[pl.ds(own, SHARD)],
            send_sem=t_send.at[i], recv_sem=t_recv.at[col], device_id=(row, to), device_id_type=MESH,
        )

    def tile_recv(i):
        source = (col + i) % COLS
        return pltpu.make_async_remote_copy(
            src_ref=coded.at[source], dst_ref=tiles_ref.at[pl.ds(pl.multiple_of(source * SHARD, SHARD), SHARD)],
            send_sem=t_send.at[i], recv_sem=t_recv.at[source], device_id=(row, source), device_id_type=MESH,
        )

    def tile_keep():
        return pltpu.make_async_copy(coded.at[col], tiles_ref.at[pl.ds(own, SHARD)], t_recv.at[col])

    def tile_start(i):
        @pl.when((col + i) % COLS >= 2)
        def _():
            tile_send(i).start()

    own_block = name(z, xl, core)

    def first(s):
        pass_on(own_block, s, 0, above).start()
        pass_on(own_block, s, 1, below).start()
        pass_on(own_block, s, 2, beside).start()
        pass_on(own_block, s, 3, sibling).start()
        have(own_block, s)

    each(0, 2, first)

    def code(t, _):
        part = held[:, pl.ds(pl.multiple_of(t * WIDTH, WIDTH), WIDTH)]
        coded[t] = (part * scale).astype(BF16)
        return 0

    lax.fori_loop(2, COLS, code, 0)

    steps = (
        (down, xl, (0, above, 4), None, 5),
        (up, xl, (1, below, 4), None, 6),
        (z, 1 - xl, None, ((above, 7), (below, 8)), 9),
        ((z + 2) % 4, xl, None, ((beside, 10),), 11),
        (down, 1 - xl, None, None, 12),
        (up, 1 - xl, None, None, 13),
        ((z + 2) % 4, 1 - xl, None, None, 14),
    )

    done = 1

    def issue(k):
        nonlocal done
        each(done, done + ISSUE[k], tile_start)
        done += ISSUE[k]

    issue(0)
    def sib_first(s):
        block = name(z, xl, other)
        arrived(block, s)
        have(block, s)

    each(0, 2, sib_first)
    for k, (z_, xl_, half, whole_sends, slot) in enumerate(steps):
        def at(s, z_=z_, xl_=xl_, half=half, whole_sends=whole_sends, slot=slot):
            block = name(z_, xl_, core)
            arrived(block, s)
            if half is not None:
                @pl.when(s == half[0])
                def _():
                    pass_on(block, s, half[2], half[1]).start()
            for target, n in whole_sends or ():
                pass_on(block, s, n, target).start()
            pass_on(block, s, slot, sibling).start()
            have(block, s)
            twin = name(z_, xl_, other)
            arrived(twin, s)
            have(twin, s)

        each(0, 2, at)
        issue(k + 1)

    def move(j, s, target):
        return pltpu.make_async_remote_copy(
            src_ref=columns.at[piece(j, s)], dst_ref=columns.at[piece(j, s)],
            send_sem=c_send.at[j, s], recv_sem=c_recv.at[j, s], device_id=target, device_id_type=MESH,
        )

    bridge = jnp.logical_not(even) & ((turn == 1) | (turn == 3))

    def relay(i, s):
        slot = jnp.where(turn == 1, 4, 6) + i
        return pltpu.make_async_remote_copy(
            src_ref=columns.at[piece(8 + i, s)], dst_ref=columns.at[piece(slot, s)],
            send_sem=c_send.at[8 + i, s], recv_sem=c_recv.at[slot, s], device_id=cross, device_id_type=MESH,
        )

    @pl.when(bridge)
    def _():
        def over(n):
            i, s = n // 2, n % 2
            move(8 + i, s, cross).wait_recv()
            relay(i, s).start()

        each(0, 4, over)

    def hop_of(j):
        ahead = (turn - start_of(j) + 4) % 4
        return jnp.where(way_of(j) == 1, ahead, (4 - ahead) % 4)

    def round_target(j):
        return place((y + way_of(j)) % 4, xh, z, xl, core)

    def carry(n):
        h, s, j = n // 16, (n // 8) % 2, n % 8

        @pl.when((hop_of(j) == h) & jnp.logical_not(even & (h == 0)))
        def _():
            move(j, s, cross).wait_recv()

            @pl.when(h < 3)
            def _():
                move(j, s, round_target(j)).start()

    each(0, 64, carry)

    @pl.when(home & even)
    def _():
        each(0, 16, lambda n: keep(core * 8 + n // 2, n % 2).wait())

    def multiply(n):
        i, k = n // 2, n % 2
        rows = pl.ds(pl.multiple_of(i * 512, 512), 512)
        cols = pl.ds(pl.multiple_of(k * 512, 512), 512)
        product = lax.dot_general(
            panel[rows, :], columns[cols, :], (((1,), (1,)), ((), ())), preferred_element_type=F32
        )
        gram_ref[rows, cols] = product * F32(WIDTH * COLS)

    each(0, 8, multiply)

    @pl.when(col >= 2)
    def _():
        tile_keep().start()
        each(1, COLS, lambda i: tile_recv(i).wait_recv())
        tile_keep().wait()

    @pl.when(col < 2)
    def _():
        def take(b):
            rows = pl.ds(pl.multiple_of(b * SHARD, SHARD), SHARD)
            tiles_ref[rows, :] = panel[rows, pl.ds(pl.multiple_of(core * WIDTH, WIDTH), WIDTH)]

        each(0, COLS, take)

    def left(i):
        @pl.when((col + i) % COLS >= 2)
        def _():
            tile_send(i).wait_send()

    each(1, COLS, left)
    each(1, COLS, lambda i: send1(i).wait_send())
    each(1, ROWS, lambda i: send2(i).wait_send())

    def gone(s):
        for n in range(15):
            pass_on(own_block, s, n, sibling).wait_send() if n != 4 else None

    each(0, 2, gone)
    pass_on(own_block, 0, 4, sibling).wait_send()
    pass_on(own_block, 1, 4, sibling).wait_send()

    @pl.when(home)
    def _():
        each(0, 16, lambda n: lead(core * 8 + n // 2, n % 2).wait_send())

    @pl.when(bridge)
    def _():
        each(0, 4, lambda n: relay(n // 2, n % 2).wait_send())

    def carried(n):
        s, j = n // 8, n % 8

        @pl.when((hop_of(j) < 3) & jnp.logical_not(even & home))
        def _():
            move(j, s, cross).wait_send()

    each(0, 16, carried)


def shards(momentum):
    dma = pltpu.SemaphoreType.DMA
    return pl.pallas_call(
        kernel,
        out_shape=(
            jax.ShapeDtypeStruct((COLS * SHARD, WIDTH), F32),
            jax.ShapeDtypeStruct((COLS * SHARD, WIDTH), BF16),
        ),
        in_specs=[pl.BlockSpec(memory_space=pltpu.HBM)],
        out_specs=(
            pl.BlockSpec(memory_space=pltpu.VMEM),
            pl.BlockSpec(memory_space=pltpu.VMEM),
        ),
        scratch_shapes=[
            pltpu.VMEM((SHARD, COLS * WIDTH), F32),
            pltpu.VMEM((COLS, SHARD, WIDTH), BF16),
            pltpu.VMEM((COLS * SHARD, WINDOW), BF16),
            pltpu.VMEM((10 * SHARD, WINDOW), BF16),
            pltpu.VMEM((COLS, 8, 128), F32),
            pltpu.VMEM((ROWS, 8, 128), F32),
            dma((8,)),
            dma((COLS,)),
            dma((COLS,)),
            dma((ROWS,)),
            dma((ROWS,)),
            dma((COLS,)),
            dma((COLS,)),
            dma((15, 2)),
            dma((COLS, 2)),
            dma((8, 2)),
            dma((10, 2)),
            dma((10, 2)),
            dma((8, 2)),
        ],
        compiler_params=pltpu.CompilerParams(
            collective_id=0, has_side_effects=True, vmem_limit_bytes=48 * MIB
        ),
        cost_estimate=pl.CostEstimate(
            flops=2 * COLS * SHARD * WIDTH * WINDOW, bytes_accessed=20 * MIB, transcendentals=0
        ),
        name="newton_gram",
    )(momentum)


def solution(mesh):
    return jax.shard_map(
        shards,
        mesh=mesh,
        in_specs=(P(("row", "col"), None),),
        out_specs=(P("row", "col"), P("row", "col")),
        check_vma=False,
    )
```

time: 559 us -> 192 us (0.34)
  the two profiles are of different devices: /device:TPU:19 before, /device:TPU:48 now
where the time goes in v1:
time: 192 us; the launch traced here: 191 us
  Pallas kernels  180 us (94%)
  local copies, waits for them, and re-layouts  10.5 us (5%)
    pallas_call x1, Pallas kernels, shards(): pl.pallas_call(kernel, out_shape=(jax.ShapeDtypeStruct((COLS * SHARD, WID...  180 us
    unnamed x2, local copies, waits for them, and re-layouts  10.5 us

profile of v1, /device:TPU:48, one launch (start us, length us, event | category | flops | bytes accessed | tf_op | source)
XLA Modules:
  0.0 191.5 jit_solution(11725232902521819188)
XLA Ops:
  0.6 180.4 %newton_gram.1 = (f32[2048,1024]{1,0:T(8,128)}, bf16[2048,1024]{1,0:T(8,128)(2,1)S(1)}) custom-call(f32[128,16384]{1,0:T(8,128)} %m_ref.1), custom_call_target="tpu_custom_call" | custom-call | flops 8589934592 | bytes 20971520 | tf_op jit(solution)/shard_map/newton_gram/pallas_call | solution.py:382
  181.0 8.4 %copy.5 = f32[2048,1024]{1,0:T(8,128)} copy(f32[2048,1024]{1,0:T(8,128)} %get-tuple-element.4) | data formatting | bytes 16777216
  189.5 2.0 %copy.6 = bf16[2048,1024]{1,0:T(8,128)(2,1)} copy(bf16[2048,1024]{1,0:T(8,128)(2,1)S(1)} %get-tuple-element.5) | data formatting | bytes 8388608

commit v2 on v1

--- a/solution.py
+++ b/solution.py
@@ -16,7 +16,12 @@
 WINDOW = 2048
 SUB = 64
 MIB = 1 << 20
-ISSUE = (2, 2, 2, 2, 2, 2, 2, 1)
+STEPS = 14
+ISSUE = (0, 0, 0, 0, 0, 0, 15, 0, 0, 0, 0, 0, 0, 0)
+PAIR = (0, 0, 1, 2, 1, 2, 3, 3)
+TWIN = (0, 1, 0, 0, 1, 1, 0, 1)
+READY = (2, 3, 4, 4, 5, 5, 6, 7)
+RANK = ((0, 1), (2, 4), (3, 5), (6, 7))
 
 
 def nothing(*_):
@@ -34,7 +39,7 @@
     y, xh = row // 2, row % 2
     z, xl, core = col // 4, (col // 2) % 2, col % 2
     other = 1 - core
-    up, down = (z + 1) % 4, (z + 3) % 4
+    up, down, opposite = (z + 1) % 4, (z + 3) % 4, (z + 2) % 4
     even = xh == xl
     turn = (y - z + 4) % 4
     home = turn == 0
@@ -150,26 +155,34 @@
     sibling = place(y, xh, z, xl, other)
 
     def start_of(j):
-        far = jnp.where(j < 6, 1, 3)
-        return jnp.where(even | (j < 4), 0, far)
+        far = jnp.where(j % 4 == 0, 1, jnp.where(j % 4 == 1, 3, 0))
+        return jnp.where(even, 0, far)
 
     def way_of(j):
-        e = jnp.where(j < 4, 1, 3)
-        m = jnp.where(j < 4, jnp.where(j < 2, 1, 3), jnp.where(j % 2 == 0, 1, 3))
-        return jnp.where(even, e, m)
-
-    def lead(block, s):
-        j = block % 8
-        near = (1 - xh, 1 - xl)
+        m = jnp.where(j % 4 < 2, jnp.where((j == 0) | (j == 5), 1, 3), jnp.where(j % 2 == 0, 1, 3))
+        return jnp.where(even, jnp.where(j % 2 == 0, 1, 3), m)
+
+    same = z // 2 == core
+    near_z = jnp.where(same, z, opposite + 1 - 2 * (opposite % 2))
+    far_z = jnp.where(same, z + 1 - 2 * (z % 2), opposite)
+
+    def slot_of(j, holder_xl=xh):
+        z_ = far_z if PAIR[j] % 2 else near_z
+        xl_ = holder_xl if PAIR[j] < 2 else 1 - holder_xl
+        return name(z_, xl_, other if TWIN[j] else core) % 8
+
+    def lead(block, s, j):
         step = jnp.where(even, way_of(j), start_of(j))
-        direct = jnp.logical_not(even) & (j < 4)
-        slot = jnp.where(even | (j < 4), j, 8 + j % 2)
+        direct = jnp.logical_not(even) & (j % 4 >= 2)
+        via = jnp.logical_not(even) & (j % 4 < 2)
+        slot = jnp.where(via, 8 + j // 4, block % 8)
+        sem = jnp.where(via, 8 + j // 4, j)
         target = place(
-            (y + step) % 4, jnp.where(direct, near[0], xh), z, jnp.where(direct, near[1], xl), core
+            (y + step) % 4, jnp.where(direct, 1 - xh, xh), z, jnp.where(direct, 1 - xl, xl), core
         )
         return pltpu.make_async_remote_copy(
             src_ref=panel.at[piece(block, s)], dst_ref=columns.at[piece(slot, s)],
-            send_sem=o_send.at[j, s], recv_sem=c_recv.at[slot, s], device_id=target, device_id_type=MESH,
+            send_sem=o_send.at[j, s], recv_sem=c_recv.at[sem, s], device_id=target, device_id_type=MESH,
         )
 
     def keep(block, s):
@@ -177,10 +190,18 @@
             panel.at[piece(block, s)], columns.at[piece(block % 8, s)], local_sem.at[block % 8, s]
         )
 
-    def have(block, s):
-        @pl.when(home & (block // 8 == core))
-        def _():
-            lead(block, s).start()
+    def mine(z_):
+        return home & (z_ // 2 == core)
+
+    def have(z_, xl_, core_, s, beside_, twin):
+        block = name(z_, xl_, core_)
+        second = jnp.where(same, z_ != z, z_ == opposite)
+        pair = 2 if beside_ else 0
+        j = jnp.where(second, RANK[pair + 1][twin], RANK[pair][twin])
+
+        @pl.when(mine(z_))
+        def _():
+            lead(block, s, j).start()
 
             @pl.when(even)
             def _():
@@ -215,7 +236,7 @@
         pass_on(own_block, s, 1, below).start()
         pass_on(own_block, s, 2, beside).start()
         pass_on(own_block, s, 3, sibling).start()
-        have(own_block, s)
+        have(z, xl, core, s, False, 0)
 
     each(0, 2, first)
 
@@ -226,72 +247,57 @@
 
     lax.fori_loop(2, COLS, code, 0)
 
-    steps = (
-        (down, xl, (0, above, 4), None, 5),
-        (up, xl, (1, below, 4), None, 6),
-        (z, 1 - xl, None, ((above, 7), (below, 8)), 9),
-        ((z + 2) % 4, xl, None, ((beside, 10),), 11),
-        (down, 1 - xl, None, None, 12),
-        (up, 1 - xl, None, None, 13),
-        ((z + 2) % 4, 1 - xl, None, None, 14),
+    arrivals = (
+        (1, down, xl, (0, above, 4), (), 5),
+        (1, up, xl, (1, below, 4), (), 6),
+        (1, z, 1 - xl, None, ((above, 7), (below, 8)), 9),
+        (2, opposite, xl, None, ((beside, 10),), 11),
+        (2, down, 1 - xl, None, (), 12),
+        (2, up, 1 - xl, None, (), 13),
+        (3, opposite, 1 - xl, None, (), 14),
     )
 
-    done = 1
-
-    def issue(k):
-        nonlocal done
-        each(done, done + ISSUE[k], tile_start)
-        done += ISSUE[k]
-
-    issue(0)
-    def sib_first(s):
-        block = name(z, xl, other)
-        arrived(block, s)
-        have(block, s)
-
-    each(0, 2, sib_first)
-    for k, (z_, xl_, half, whole_sends, slot) in enumerate(steps):
-        def at(s, z_=z_, xl_=xl_, half=half, whole_sends=whole_sends, slot=slot):
+    def gather(z_, xl_, half, sends, slot, beside_):
+        def at(s):
             block = name(z_, xl_, core)
             arrived(block, s)
             if half is not None:
+
                 @pl.when(s == half[0])
                 def _():
                     pass_on(block, s, half[2], half[1]).start()
-            for target, n in whole_sends or ():
+
+            for target, n in sends:
                 pass_on(block, s, n, target).start()
             pass_on(block, s, slot, sibling).start()
-            have(block, s)
-            twin = name(z_, xl_, other)
-            arrived(twin, s)
-            have(twin, s)
+            have(z_, xl_, core, s, beside_, 0)
 
         each(0, 2, at)
-        issue(k + 1)
-
-    def move(j, s, target):
-        return pltpu.make_async_remote_copy(
-            src_ref=columns.at[piece(j, s)], dst_ref=columns.at[piece(j, s)],
+
+    def from_sibling(z_, xl_, beside_):
+        @pl.when(mine(z_))
+        def _():
+            def at(s):
+                arrived(name(z_, xl_, other), s)
+                have(z_, xl_, other, s, beside_, 1)
+
+            each(0, 2, at)
+
+    def move(slot, j, s, target):
+        return pltpu.make_async_remote_copy(
+            src_ref=columns.at[piece(slot, s)], dst_ref=columns.at[piece(slot, s)],
             send_sem=c_send.at[j, s], recv_sem=c_recv.at[j, s], device_id=target, device_id_type=MESH,
         )
 
-    bridge = jnp.logical_not(even) & ((turn == 1) | (turn == 3))
-
-    def relay(i, s):
-        slot = jnp.where(turn == 1, 4, 6) + i
-        return pltpu.make_async_remote_copy(
-            src_ref=columns.at[piece(8 + i, s)], dst_ref=columns.at[piece(slot, s)],
-            send_sem=c_send.at[8 + i, s], recv_sem=c_recv.at[slot, s], device_id=cross, device_id_type=MESH,
-        )
-
-    @pl.when(bridge)
-    def _():
-        def over(n):
-            i, s = n // 2, n % 2
-            move(8 + i, s, cross).wait_recv()
-            relay(i, s).start()
-
-        each(0, 4, over)
+    def bridge(j):
+        return jnp.logical_not(even) & (turn == (3 if j % 4 else 1))
+
+    def relay(j, s):
+        slot = slot_of(j, 1 - xh)
+        return pltpu.make_async_remote_copy(
+            src_ref=columns.at[piece(8 + j // 4, s)], dst_ref=columns.at[piece(slot, s)],
+            send_sem=c_send.at[8 + j // 4, s], recv_sem=c_recv.at[j, s], device_id=cross, device_id_type=MESH,
+        )
 
     def hop_of(j):
         ahead = (turn - start_of(j) + 4) % 4
@@ -300,33 +306,83 @@
     def round_target(j):
         return place((y + way_of(j)) % 4, xh, z, xl, core)
 
-    def carry(n):
-        h, s, j = n // 16, (n // 8) % 2, n % 8
-
-        @pl.when((hop_of(j) == h) & jnp.logical_not(even & (h == 0)))
-        def _():
-            move(j, s, cross).wait_recv()
-
-            @pl.when(h < 3)
-            def _():
-                move(j, s, round_target(j)).start()
-
-    each(0, 64, carry)
+    def carry(step):
+        for j in range(8):
+            late = step - READY[j] + jnp.where(same, 2, 0)
+            via = j % 4 < 2
+            if via and 0 <= step - READY[j] <= 2:
+
+                @pl.when(bridge(j) & (late == 2))
+                def _(j=j):
+                    def at(s):
+                        move(8 + j // 4, 8 + j // 4, s, cross).wait_recv()
+                        relay(j, s).start()
+
+                    each(0, 2, at)
+
+            if step - READY[j] in (0, 2, 4, 6, 8):
+                hop = hop_of(j)
+                begun = jnp.where(even, 0, 4 if via else 2)
+                go = (late == begun + 2 * hop) & (hop < 3) & jnp.logical_not(even & home)
+
+                @pl.when(go)
+                def _(j=j):
+                    def at(s):
+                        move(slot_of(j), j, s, cross).wait_recv()
+                        move(slot_of(j), j, s, round_target(j)).start()
+
+                    each(0, 2, at)
+
+    done = 1
+    for step in range(STEPS):
+        if step == 1:
+            from_sibling(z, xl, False)
+        for lv, z_, xl_, half, sends, slot in arrivals:
+            if 2 * lv == step:
+                gather(z_, xl_, half, sends, slot, xl_ is not xl)
+        for lv, z_, xl_, half, sends, slot in arrivals:
+            if 2 * lv + 1 == step:
+                from_sibling(z_, xl_, xl_ is not xl)
+        carry(step)
+        each(done, done + ISSUE[step], tile_start)
+        done += ISSUE[step]
+
+    def last(j):
+        @pl.when(hop_of(j) == 3)
+        def _():
+            def at(s):
+                move(slot_of(j), j, s, cross).wait_recv()
+
+            each(0, 2, at)
+
+    def rest(n):
+        block, s = n // 2, n % 2
+
+        @pl.when((block % 2 == other) & jnp.logical_not(mine(block // 4)))
+        def _():
+            arrived(block, s)
+
+    each(0, 2 * COLS, rest)
 
     @pl.when(home & even)
     def _():
         each(0, 16, lambda n: keep(core * 8 + n // 2, n % 2).wait())
 
-    def multiply(n):
-        i, k = n // 2, n % 2
-        rows = pl.ds(pl.multiple_of(i * 512, 512), 512)
-        cols = pl.ds(pl.multiple_of(k * 512, 512), 512)
-        product = lax.dot_general(
-            panel[rows, :], columns[cols, :], (((1,), (1,)), ((), ())), preferred_element_type=F32
-        )
-        gram_ref[rows, cols] = product * F32(WIDTH * COLS)
-
-    each(0, 8, multiply)
+    for pair in (0, 1, 2, 3):
+        for j in range(8):
+            if PAIR[j] == pair:
+                last(j)
+        first_slot = slot_of(PAIR.index(pair)) // 2 * 2
+        rows = pl.ds(pl.multiple_of(first_slot * SHARD, 2 * SHARD), 2 * SHARD)
+
+        def multiply(i, rows=rows):
+            across = pl.ds(pl.multiple_of(i * 1024, 1024), 1024)
+            product = lax.dot_general(
+                panel[across, :], columns[rows, :], (((1,), (1,)), ((), ())), preferred_element_type=F32
+            )
+            gram_ref[across, rows] = product * F32(WIDTH * COLS)
+
+        each(0, 2, multiply)
 
     @pl.when(col >= 2)
     def _():
@@ -361,20 +417,18 @@
 
     @pl.when(home)
     def _():
-        each(0, 16, lambda n: lead(core * 8 + n // 2, n % 2).wait_send())
-
-    @pl.when(bridge)
-    def _():
-        each(0, 4, lambda n: relay(n // 2, n % 2).wait_send())
-
-    def carried(n):
-        s, j = n // 8, n % 8
+        each(0, 16, lambda n: lead(core * 8 + n // 2, n % 2, n // 2).wait_send())
+
+    for j in range(8):
+        if j % 4 < 2:
+
+            @pl.when(bridge(j))
+            def _(j=j):
+                each(0, 2, lambda s: relay(j, s).wait_send())
 
         @pl.when((hop_of(j) < 3) & jnp.logical_not(even & home))
-        def _():
-            move(j, s, cross).wait_send()
-
-    each(0, 16, carried)
+        def _(j=j):
+            each(0, 2, lambda s: move(slot_of(j), j, s, cross).wait_send())
 
 
 def shards(momentum):
@@ -382,8 +436,8 @@
     return pl.pallas_call(
         kernel,
         out_shape=(
-            jax.ShapeDtypeStruct((COLS * SHARD, WIDTH), F32),
-            jax.ShapeDtypeStruct((COLS * SHARD, WIDTH), BF16),
+            pltpu.VMEM((COLS * SHARD, WIDTH), F32),
+            pltpu.VMEM((COLS * SHARD, WIDTH), BF16),
         ),
         in_specs=[pl.BlockSpec(memory_space=pltpu.HBM)],
         out_specs=(
@@ -412,7 +466,7 @@
             dma((8, 2)),
         ],
         compiler_params=pltpu.CompilerParams(
-            collective_id=0, has_side_effects=True, vmem_limit_bytes=48 * MIB
+            collective_id=0, has_side_effects=True, vmem_limit_bytes=36 * MIB
         ),
         cost_estimate=pl.CostEstimate(
             flops=2 * COLS * SHARD * WIDTH * WINDOW, bytes_accessed=20 * MIB, transcendentals=0

time: 192 us -> 120 us (0.62)
  the two profiles are of different devices: /device:TPU:48 before, /device:TPU:19 now
where the time goes in v2:
time: 120 us; the launch traced here: 118 us
  Pallas kernels  112 us (93%)
  local copies, waits for them, and re-layouts  5.41 us (5%)
    pallas_call x1, Pallas kernels, shards(): pl.pallas_call(kernel, out_shape=(pltpu.VMEM((COLS * SHARD, WIDTH), F32),...  112 us
    unnamed x2, local copies, waits for them, and re-layouts  5.41 us

profile of v2, /device:TPU:19, one launch (start us, length us, event | category | flops | bytes accessed | tf_op | source)
XLA Modules:
  0.0 118.4 jit_solution(13133574757109629428)
XLA Ops:
  0.6 112.4 %newton_gram.1 = (f32[2048,1024]{1,0:T(8,128)S(1)}, bf16[2048,1024]{1,0:T(8,128)(2,1)S(1)}) custom-call(f32[128,16384]{1,0:T(8,128)} %m_ref.1), custom_call_target="tpu_custom_call" | custom-call | flops 8589934592 | bytes 20971520 | tf_op jit(solution)/shard_map/newton_gram/pallas_call | solution.py:436
  113.0 3.4 %copy.5 = f32[2048,1024]{1,0:T(8,128)} copy(f32[2048,1024]{1,0:T(8,128)S(1)} %get-tuple-element.2) | data formatting | bytes 16777216
  116.4 2.0 %copy.6 = bf16[2048,1024]{1,0:T(8,128)(2,1)} copy(bf16[2048,1024]{1,0:T(8,128)(2,1)S(1)} %get-tuple-element.3) | data formatting | bytes 8388608

commit v3 on v2

--- a/solution.py
+++ b/solution.py
@@ -14,13 +14,20 @@
 SHARD = 128
 WIDTH = 1024
 WINDOW = 2048
-SUB = 64
+PIECES = 4
+SUB = SHARD // PIECES
 MIB = 1 << 20
-STEPS = 14
-ISSUE = (0, 0, 0, 0, 0, 0, 15, 0, 0, 0, 0, 0, 0, 0)
+STEPS = 12
+ISSUE = (0, 0, 0, 0, 0, 15, 0, 0, 0, 0, 0, 0)
+TURNS = tuple(
+    (dz, dx, dc)
+    for dc in (0, 1)
+    for dz, dx in ((1, 0), (3, 0), (0, 1), (2, 1), (1, 1), (3, 1), (2, 0), (0, 0))
+    if (dz, dx, dc) != (0, 0, 0)
+)
 PAIR = (0, 0, 1, 2, 1, 2, 3, 3)
 TWIN = (0, 1, 0, 0, 1, 1, 0, 1)
-READY = (2, 3, 4, 4, 5, 5, 6, 7)
+BASE = (3, 3, 5, 5, 7, 7, 8, 8)
 RANK = ((0, 1), (2, 4), (3, 5), (6, 7))
 
 
@@ -207,8 +214,12 @@
             def _():
                 keep(block, s).start()
 
+    def partner(i):
+        dz, dx, dc = TURNS[i]
+        return name((z + dz) % 4, 1 - xl if dx else xl, other if dc else core)
+
     def tile_send(i):
-        to = (col + i) % COLS
+        to = partner(i)
         return pltpu.make_async_remote_copy(
             src_ref=coded.at[to], dst_ref=tiles_ref.at[pl.ds(own, SHARD)],
             send_sem=t_send.at[i], recv_sem=t_recv.at[col], device_id=(row, to), device_id_type=MESH,
@@ -225,7 +236,7 @@
         return pltpu.make_async_copy(coded.at[col], tiles_ref.at[pl.ds(own, SHARD)], t_recv.at[col])
 
     def tile_start(i):
-        @pl.when((col + i) % COLS >= 2)
+        @pl.when(partner(i) >= 2)
         def _():
             tile_send(i).start()
 
@@ -238,7 +249,7 @@
         pass_on(own_block, s, 3, sibling).start()
         have(z, xl, core, s, False, 0)
 
-    each(0, 2, first)
+    each(0, PIECES, first)
 
     def code(t, _):
         part = held[:, pl.ds(pl.multiple_of(t * WIDTH, WIDTH), WIDTH)]
@@ -248,13 +259,13 @@
     lax.fori_loop(2, COLS, code, 0)
 
     arrivals = (
-        (1, down, xl, (0, above, 4), (), 5),
-        (1, up, xl, (1, below, 4), (), 6),
-        (1, z, 1 - xl, None, ((above, 7), (below, 8)), 9),
-        (2, opposite, xl, None, ((beside, 10),), 11),
-        (2, down, 1 - xl, None, (), 12),
-        (2, up, 1 - xl, None, (), 13),
-        (3, opposite, 1 - xl, None, (), 14),
+        (2, down, xl, (0, above, 4), (), 5),
+        (2, up, xl, (1, below, 4), (), 6),
+        (2, z, 1 - xl, None, ((above, 7), (below, 8)), 9),
+        (4, opposite, xl, None, ((beside, 10),), 11),
+        (5, down, 1 - xl, None, (), 12),
+        (5, up, 1 - xl, None, (), 13),
+        (6, opposite, 1 - xl, None, (), 14),
     )
 
     def gather(z_, xl_, half, sends, slot, beside_):
@@ -263,7 +274,7 @@
             arrived(block, s)
             if half is not None:
 
-                @pl.when(s == half[0])
+                @pl.when(s * 2 // PIECES == half[0])
                 def _():
                     pass_on(block, s, half[2], half[1]).start()
 
@@ -272,7 +283,7 @@
             pass_on(block, s, slot, sibling).start()
             have(z_, xl_, core, s, beside_, 0)
 
-        each(0, 2, at)
+        each(0, PIECES, at)
 
     def from_sibling(z_, xl_, beside_):
         @pl.when(mine(z_))
@@ -281,7 +292,7 @@
                 arrived(name(z_, xl_, other), s)
                 have(z_, xl_, other, s, beside_, 1)
 
-            each(0, 2, at)
+            each(0, PIECES, at)
 
     def move(slot, j, s, target):
         return pltpu.make_async_remote_copy(
@@ -308,22 +319,22 @@
 
     def carry(step):
         for j in range(8):
-            late = step - READY[j] + jnp.where(same, 2, 0)
+            late = step - BASE[j] + jnp.where(same, 2, 0)
             via = j % 4 < 2
-            if via and 0 <= step - READY[j] <= 2:
-
-                @pl.when(bridge(j) & (late == 2))
+            if via and -1 <= step - BASE[j] <= 1:
+
+                @pl.when(bridge(j) & (late == 1))
                 def _(j=j):
                     def at(s):
                         move(8 + j // 4, 8 + j // 4, s, cross).wait_recv()
                         relay(j, s).start()
 
-                    each(0, 2, at)
-
-            if step - READY[j] in (0, 2, 4, 6, 8):
+                    each(0, PIECES, at)
+
+            if -1 <= step - BASE[j] <= (4 if via else 3):
                 hop = hop_of(j)
-                begun = jnp.where(even, 0, 4 if via else 2)
-                go = (late == begun + 2 * hop) & (hop < 3) & jnp.logical_not(even & home)
+                begun = jnp.where(even, 0, 2 if via else 1)
+                go = (late == begun + hop) & (hop < 3) & jnp.logical_not(even & home)
 
                 @pl.when(go)
                 def _(j=j):
@@ -331,21 +342,7 @@
                         move(slot_of(j), j, s, cross).wait_recv()
                         move(slot_of(j), j, s, round_target(j)).start()
 
-                    each(0, 2, at)
-
-    done = 1
-    for step in range(STEPS):
-        if step == 1:
-            from_sibling(z, xl, False)
-        for lv, z_, xl_, half, sends, slot in arrivals:
-            if 2 * lv == step:
-                gather(z_, xl_, half, sends, slot, xl_ is not xl)
-        for lv, z_, xl_, half, sends, slot in arrivals:
-            if 2 * lv + 1 == step:
-                from_sibling(z_, xl_, xl_ is not xl)
-        carry(step)
-        each(done, done + ISSUE[step], tile_start)
-        done += ISSUE[step]
+                    each(0, PIECES, at)
 
     def last(j):
         @pl.when(hop_of(j) == 3)
@@ -353,36 +350,56 @@
             def at(s):
                 move(slot_of(j), j, s, cross).wait_recv()
 
-            each(0, 2, at)
-
-    def rest(n):
-        block, s = n // 2, n % 2
-
-        @pl.when((block % 2 == other) & jnp.logical_not(mine(block // 4)))
-        def _():
-            arrived(block, s)
-
-    each(0, 2 * COLS, rest)
-
-    @pl.when(home & even)
-    def _():
-        each(0, 16, lambda n: keep(core * 8 + n // 2, n % 2).wait())
-
-    for pair in (0, 1, 2, 3):
+            each(0, PIECES, at)
+
+    def product(pair):
         for j in range(8):
             if PAIR[j] == pair:
                 last(j)
         first_slot = slot_of(PAIR.index(pair)) // 2 * 2
         rows = pl.ds(pl.multiple_of(first_slot * SHARD, 2 * SHARD), 2 * SHARD)
 
-        def multiply(i, rows=rows):
+        def multiply(i):
             across = pl.ds(pl.multiple_of(i * 1024, 1024), 1024)
-            product = lax.dot_general(
+            block = lax.dot_general(
                 panel[across, :], columns[rows, :], (((1,), (1,)), ((), ())), preferred_element_type=F32
             )
-            gram_ref[across, rows] = product * F32(WIDTH * COLS)
+            gram_ref[across, rows] = block * F32(WIDTH * COLS)
 
         each(0, 2, multiply)
+
+    done = 0
+    for step in range(STEPS):
+        if step == 1:
+            from_sibling(z, xl, False)
+        for at_step, z_, xl_, half, sends, slot in arrivals:
+            if at_step == step:
+                gather(z_, xl_, half, sends, slot, xl_ is not xl)
+        for at_step, z_, xl_, half, sends, slot in arrivals:
+            if at_step == step:
+                from_sibling(z_, xl_, xl_ is not xl)
+        carry(step)
+        if step == 8:
+            def rest(n):
+                block, s = n // PIECES, n % PIECES
+
+                @pl.when((block % 2 == other) & jnp.logical_not(mine(block // 4)))
+                def _():
+                    arrived(block, s)
+
+            each(0, PIECES * COLS, rest)
+
+            @pl.when(home & even)
+            def _():
+                each(0, 8 * PIECES, lambda n: keep(core * 8 + n // PIECES, n % PIECES).wait())
+        if step == 9:
+            product(0)
+        for i in range(done, done + ISSUE[step]):
+            tile_start(i)
+        done += ISSUE[step]
+
+    for pair in (1, 2, 3):
+        product(pair)
 
     @pl.when(col >= 2)
     def _():
@@ -398,37 +415,35 @@
 
         each(0, COLS, take)
 
-    def left(i):
-        @pl.when((col + i) % COLS >= 2)
-        def _():
+    for i in range(len(TURNS)):
+
+        @pl.when(partner(i) >= 2)
+        def _(i=i):
             tile_send(i).wait_send()
 
-    each(1, COLS, left)
     each(1, COLS, lambda i: send1(i).wait_send())
     each(1, ROWS, lambda i: send2(i).wait_send())
 
     def gone(s):
         for n in range(15):
-            pass_on(own_block, s, n, sibling).wait_send() if n != 4 else None
-
-    each(0, 2, gone)
-    pass_on(own_block, 0, 4, sibling).wait_send()
-    pass_on(own_block, 1, 4, sibling).wait_send()
+            pass_on(own_block, s, n, sibling).wait_send()
+
+    each(0, PIECES, gone)
 
     @pl.when(home)
     def _():
-        each(0, 16, lambda n: lead(core * 8 + n // 2, n % 2, n // 2).wait_send())
+        each(0, 8 * PIECES, lambda n: lead(core * 8 + n // PIECES, n % PIECES, n // PIECES).wait_send())
 
     for j in range(8):
         if j % 4 < 2:
 
             @pl.when(bridge(j))
             def _(j=j):
-                each(0, 2, lambda s: relay(j, s).wait_send())
+                each(0, PIECES, lambda s: relay(j, s).wait_send())
 
         @pl.when((hop_of(j) < 3) & jnp.logical_not(even & home))
         def _(j=j):
-            each(0, 2, lambda s: move(slot_of(j), j, s, cross).wait_send())
+            each(0, PIECES, lambda s: move(slot_of(j), j, s, cross).wait_send())
 
 
 def shards(momentum):
@@ -458,12 +473,12 @@
             dma((ROWS,)),
             dma((COLS,)),
             dma((COLS,)),
-            dma((15, 2)),
-            dma((COLS, 2)),
-            dma((8, 2)),
-            dma((10, 2)),
-            dma((10, 2)),
-            dma((8, 2)),
+            dma((15, PIECES)),
+            dma((COLS, PIECES)),
+            dma((8, PIECES)),
+            dma((10, PIECES)),
+            dma((10, PIECES)),
+            dma((8, PIECES)),
         ],
         compiler_params=pltpu.CompilerParams(
             collective_id=0, has_side_effects=True, vmem_limit_bytes=36 * MIB

time: 120 us -> 118 us (0.983); the launches traced: 118 us -> 118 us
  no operation moved by 1% of the time
where the time goes in v3:
time: 118 us
  Pallas kernels  112 us (95%)
  local copies, waits for them, and re-layouts  5.41 us (5%)
    pallas_call x1, Pallas kernels, shards(): pl.pallas_call(kernel, out_shape=(pltpu.VMEM((COLS * SHARD, WIDTH), F32),...  112 us
    unnamed x2, local copies, waits for them, and re-layouts  5.41 us

profile of v3, /device:TPU:19, one launch (start us, length us, event | category | flops | bytes accessed | tf_op | source)
XLA Modules:
  0.0 118.3 jit_solution(14709907928026539077)
XLA Ops:
  0.6 112.3 %newton_gram.1 = (f32[2048,1024]{1,0:T(8,128)S(1)}, bf16[2048,1024]{1,0:T(8,128)(2,1)S(1)}) custom-call(f32[128,16384]{1,0:T(8,128)} %m_ref.1), custom_call_target="tpu_custom_call" | custom-call | flops 8589934592 | bytes 20971520 | tf_op jit(solution)/shard_map/newton_gram/pallas_call | solution.py:451
  112.9 3.4 %copy.5 = f32[2048,1024]{1,0:T(8,128)} copy(f32[2048,1024]{1,0:T(8,128)S(1)} %get-tuple-element.2) | data formatting | bytes 16777216
  116.3 2.0 %copy.6 = bf16[2048,1024]{1,0:T(8,128)(2,1)} copy(bf16[2048,1024]{1,0:T(8,128)(2,1)S(1)} %get-tuple-element.3) | data formatting | bytes 8388608

commit v4 on v3

--- a/solution.py
+++ b/solution.py
@@ -251,13 +251,6 @@
 
     each(0, PIECES, first)
 
-    def code(t, _):
-        part = held[:, pl.ds(pl.multiple_of(t * WIDTH, WIDTH), WIDTH)]
-        coded[t] = (part * scale).astype(BF16)
-        return 0
-
-    lax.fori_loop(2, COLS, code, 0)
-
     arrivals = (
         (2, down, xl, (0, above, 4), (), 5),
         (2, up, xl, (1, below, 4), (), 6),
@@ -367,6 +360,11 @@
             gram_ref[across, rows] = block * F32(WIDTH * COLS)
 
         each(0, 2, multiply)
+
+    def code(t, _):
+        part = held[:, pl.ds(pl.multiple_of(t * WIDTH, WIDTH), WIDTH)]
+        coded[t] = (part * scale).astype(BF16)
+        return 0
 
     done = 0
     for step in range(STEPS):
@@ -379,6 +377,8 @@
             if at_step == step:
                 from_sibling(z_, xl_, xl_ is not xl)
         carry(step)
+        if step == 2:
+            lax.fori_loop(2, COLS, code, 0)
         if step == 8:
             def rest(n):
                 block, s = n // PIECES, n % PIECES
@@ -392,13 +392,11 @@
             @pl.when(home & even)
             def _():
                 each(0, 8 * PIECES, lambda n: keep(core * 8 + n // PIECES, n % PIECES).wait())
-        if step == 9:
-            product(0)
         for i in range(done, done + ISSUE[step]):
             tile_start(i)
         done += ISSUE[step]
 
-    for pair in (1, 2, 3):
+    for pair in (0, 1, 2, 3):
         product(pair)
 
     @pl.when(col >= 2)

time: 118 us -> 117 us (level)
    pallas_call x1, Pallas kernels: 112 us -> 111 us  [shards(): pl.pallas_call(kernel, out_shape=(pltpu.VMEM((COLS * SHARD, WIDTH), F32),...]
where the time goes in v4:
time: 117 us
  Pallas kernels  111 us (95%)
  local copies, waits for them, and re-layouts  5.41 us (5%)
    pallas_call x1, Pallas kernels, shards(): pl.pallas_call(kernel, out_shape=(pltpu.VMEM((COLS * SHARD, WIDTH), F32),...  111 us
    unnamed x2, local copies, waits for them, and re-layouts  5.41 us

profile of v4, /device:TPU:19, one launch (start us, length us, event | category | flops | bytes accessed | tf_op | source)
XLA Modules:
  0.0 116.9 jit_solution(144231566426782288)
XLA Ops:
  0.6 110.8 %newton_gram.1 = (f32[2048,1024]{1,0:T(8,128)S(1)}, bf16[2048,1024]{1,0:T(8,128)(2,1)S(1)}) custom-call(f32[128,16384]{1,0:T(8,128)} %m_ref.1), custom_call_target="tpu_custom_call" | custom-call | flops 8589934592 | bytes 20971520 | tf_op jit(solution)/shard_map/newton_gram/pallas_call | solution.py:449
  111.5 3.4 %copy.5 = f32[2048,1024]{1,0:T(8,128)} copy(f32[2048,1024]{1,0:T(8,128)S(1)} %get-tuple-element.2) | data formatting | bytes 16777216
  114.9 2.0 %copy.6 = bf16[2048,1024]{1,0:T(8,128)(2,1)} copy(bf16[2048,1024]{1,0:T(8,128)(2,1)S(1)} %get-tuple-element.3) | data formatting | bytes 8388608

commit v5 on v4

--- a/solution.py
+++ b/solution.py
@@ -18,11 +18,12 @@
 SUB = SHARD // PIECES
 MIB = 1 << 20
 STEPS = 12
-ISSUE = (0, 0, 0, 0, 0, 15, 0, 0, 0, 0, 0, 0)
+ISSUE = (0, 0, 0, 0, 0, 7, 8, 0, 0, 0, 0, 0)
 TURNS = tuple(
     (dz, dx, dc)
+    for dx in (0, 1)
     for dc in (0, 1)
-    for dz, dx in ((1, 0), (3, 0), (0, 1), (2, 1), (1, 1), (3, 1), (2, 0), (0, 0))
+    for dz in (1, 3, 2, 0)
     if (dz, dx, dc) != (0, 0, 0)
 )
 PAIR = (0, 0, 1, 2, 1, 2, 3, 3)

time: 117 us -> 121 us (1.034)
  the two profiles are of different devices: /device:TPU:19 before, /device:TPU:71 now
where the time goes in v5:
time: 121 us
  Pallas kernels  115 us (95%)
  local copies, waits for them, and re-layouts  5.41 us (4%)
    pallas_call x1, Pallas kernels, shards(): pl.pallas_call(kernel, out_shape=(pltpu.VMEM((COLS * SHARD, WIDTH), F32),...  115 us
    unnamed x2, local copies, waits for them, and re-layouts  5.41 us

profile of v5, /device:TPU:71, one launch (start us, length us, event | category | flops | bytes accessed | tf_op | source)
XLA Modules:
  0.0 121.1 jit_solution(1637804149748978200)
XLA Ops:
  0.6 115.0 %newton_gram.1 = (f32[2048,1024]{1,0:T(8,128)S(1)}, bf16[2048,1024]{1,0:T(8,128)(2,1)S(1)}) custom-call(f32[128,16384]{1,0:T(8,128)} %m_ref.1), custom_call_target="tpu_custom_call" | custom-call | flops 8589934592 | bytes 20971520 | tf_op jit(solution)/shard_map/newton_gram/pallas_call | solution.py:450
  115.7 3.4 %copy.5 = f32[2048,1024]{1,0:T(8,128)} copy(f32[2048,1024]{1,0:T(8,128)S(1)} %get-tuple-element.2) | data formatting | bytes 16777216
  119.1 2.0 %copy.6 = bf16[2048,1024]{1,0:T(8,128)(2,1)} copy(bf16[2048,1024]{1,0:T(8,128)(2,1)S(1)} %get-tuple-element.3) | data formatting | bytes 8388608
